TPU v7x, 32 devices: a whole 2x2x4 slice. The times are simulated.
32 devices in a mesh: groups: 2 (over y), row: 4 (over z), col: 2 (over x), chan: 2 (over core).
Axes of the slice: x: 2, y: 2, z: 4, core: 2. Of those that a mesh axis runs over, the one named last changes fastest.
Arguments:
- pair_act: bfloat16 [192, 96, 128], P(('groups', 'row'), 'col'), parts along dimension 0, may hold values from -40 to 40
- res_mask: int32 [192], P('groups'), parts along dimension 0, may hold values 0 or 1
- in_gain: float32 [2, 128], replicated, may hold values from 0.25 to 1.75
- in_bias: float32 [2, 128], replicated, may hold values from -1.5 to 1.5
- w_proj: bfloat16 [2, 4, 128, 128], replicated, may hold values from -0.5 to 0.5
- w_gate: bfloat16 [2, 128, 128], replicated, may hold values from -0.5 to 0.5
- out_gain: float32 [2, 128], replicated, may hold values from 0.25 to 1.75
- out_bias: float32 [2, 128], replicated, may hold values from -1.5 to 1.5
- w_out: bfloat16 [2, 128, 128], replicated, may hold values from -0.5 to 0.5
Outputs:
- pair_out: float32 [192, 96, 128], P(('groups', 'row', 'chan'), 'col'), parts along dimension 0
There are 2 independent parts, one for each index of `groups`. A program takes and returns all parts, laid end to end along the dimension named above; an argument that names none is the same for every part. Nothing has to cross between parts.
All inputs are finite; a program needn't handle non-finite values.
Results may differ from a plain program's by a relative error of at most 0.0015.
Values may be sent and summed in bfloat16 or wider, within the bound.
A program may use at most 128 MiB of HBM per device.

v0:
```python
import jax
import jax.numpy as jnp
from jax import lax
from jax.sharding import PartitionSpec as P

EPSILON = 1e-05


def layer_norm(values, gain_vec, offset, norm_axis):
    average = jnp.mean(values, axis=norm_axis, keepdims=True)
    centred = values - average
    variance = jnp.mean(centred * centred, axis=norm_axis, keepdims=True)
    return centred * lax.rsqrt(variance + EPSILON) * gain_vec + offset


def project_pair(normed, weights, mask_tile):
    projected = jnp.einsum("rsd,wde->wers", normed, weights, preferred_element_type=jnp.float32)
    left_side = (mask_tile * jax.nn.sigmoid(projected[0]) * projected[1]).astype(jnp.bfloat16)
    right_side = (mask_tile * jax.nn.sigmoid(projected[2]) * projected[3]).astype(jnp.bfloat16)
    return (left_side, right_side)


def triangle_core(left_side, right_side, incoming):
    full_left = lax.all_gather(left_side, "col", axis=2, tiled=True)
    if incoming:
        summed = jnp.einsum(
            "cki,ckj->cij", full_left, right_side, preferred_element_type=jnp.float32
        )
    else:
        right_rows = lax.all_to_all(right_side, "col", split_axis=1, concat_axis=2, tiled=True)
        summed = jnp.einsum(
            "cik,cjk->cij", full_left, right_rows, preferred_element_type=jnp.float32
        )
    return summed.astype(jnp.bfloat16)


def finish_layer(update, normed, pair_now, w_gate_layer, gain_vec, offset, w_out_layer):
    gate_act = jax.nn.sigmoid(
        jnp.einsum("rsd,dz->rsz", normed, w_gate_layer, preferred_element_type=jnp.float32)
    )
    unit_act = layer_norm(
        update.astype(jnp.float32), gain_vec[:, None, None], offset[:, None, None], 0
    ).astype(jnp.bfloat16)
    mixed_out = jnp.einsum("ers,ez->rsz", unit_act, w_out_layer, preferred_element_type=jnp.float32)
    return pair_now + gate_act * mixed_out


def local(pair_act, res_mask, in_gain, in_bias, w_proj, w_gate, out_gain, out_bias, w_out):
    tile_rows = pair_act.shape[0]
    tile_cols = pair_act.shape[1]
    core_count = lax.axis_size("chan")
    half_rows = tile_rows // core_count
    width_h = w_proj.shape[3]
    half_width = width_h // core_count
    core_index = lax.axis_index("chan")
    own_start = core_index * half_rows
    mask_float = res_mask.astype(jnp.float32)
    row_start = lax.axis_index("row") * tile_rows
    col_mask = lax.dynamic_slice_in_dim(mask_float, lax.axis_index("col") * tile_cols, tile_cols)
    pair_now = pair_act.astype(jnp.float32)
    row_mask = lax.dynamic_slice_in_dim(mask_float, row_start, tile_rows)
    mask_tile = row_mask[:, None] * col_mask[None, :]
    for layer_no in range(2):
        incoming = layer_no == 1
        gain_vec = out_gain[layer_no]
        offset = out_bias[layer_no]
        w_out_layer = w_out[layer_no]
        if incoming:
            pair_now = lax.all_gather(pair_now, "chan", axis=0, tiled=True)
        normed = layer_norm(pair_now, in_gain[layer_no], in_bias[layer_no], 2).astype(jnp.bfloat16)
        weights = lax.dynamic_slice_in_dim(w_proj[layer_no], core_index * half_width, half_width, 2)
        left_side, right_side = project_pair(normed, weights, mask_tile)
        left_side, right_side = (
            lax.all_to_all(left_side, "row", split_axis=0, concat_axis=1, tiled=True),
            lax.all_to_all(right_side, "row", split_axis=0, concat_axis=1, tiled=True),
        )
        product = triangle_core(left_side, right_side, incoming)
        returned = lax.all_to_all(product, "row", split_axis=1, concat_axis=0, tiled=True)
        update = lax.all_to_all(returned, "chan", split_axis=1, concat_axis=0, tiled=True)
        normed = lax.dynamic_slice_in_dim(normed, own_start, half_rows, 0)
        pair_now = lax.dynamic_slice_in_dim(pair_now, own_start, half_rows, 0)
        pair_now = finish_layer(
            update, normed, pair_now, w_gate[layer_no], gain_vec, offset, w_out_layer
        )
    return pair_now


def solution(mesh):
    in_specs = (P(("groups", "row"), "col", None), P("groups"), P(), P(), P(), P(), P(), P(), P())
    out_specs = P(("groups", "row", "chan"), "col", None)
    return jax.shard_map(local, mesh=mesh, in_specs=in_specs, out_specs=out_specs, check_vma=False)
```

profile of v0, /device:TPU:0, one launch (start us, length us, event | category | flops | bytes accessed | tf_op | source)
XLA Modules:
  0.0 107.0 jit_solution(12583398986830918049)
XLA Ops:
  0.0 0.7 convert_element_type.68
  0.8 1.2 %convert_reduce_fusion = f32[24,48]{1,0:T(8,128)S(1)} fusion(bf16[24,48,128]{2,1,0:T(8,128)(2,1)} %param.9), kind=kLoop, calls=%fused_computation.72 | loop fusion | flops 293760 | bytes 299520 | tf_op jit(solution)/shard_map/reduce_sum | solution.py:10
  2.0 1.4 %multiply_reduce_fusion.1 = f32[24,48]{1,0:T(8,128)S(1)} fusion(bf16[24,48,128]{2,1,0:T(8,128)(2,1)} %param.9, f32[24,48]{1,0:T(8,128)S(1)} %broadcast_multiply_fusion.2), kind=kLoop, calls=%fused_computation.71 | loop fusion | flops 588672 | bytes 304128 | tf_op jit(solution)/shard_map/reduce_sum | solution.py:12
  3.4 1.0 fusion.74
  4.5 0.8 slice_bitcast_fusion.4
  5.2 1.3 %add_convert_fusion.1 = bf16[24,48,128]{2,1,0:T(8,128)(2,1)S(1)} fusion(bf16[24,48,128]{2,1,0:T(8,128)(2,1)} %param.9, f32[128]{0:T(128)S(1)} %get-tuple-element.18, f32[128]{0:T(128)S(1)} %get-tuple-element.19, f32[24,48]{1,0:T(8,128)S(1)} %add_rsqrt_fusion.1, f32[24,48]{1,0:T(8,128)S(1)} %broadcast_multiply_fusion.2), kind=kLoop, calls=%fused_computation.70 | loop fusion | flops 884736 | bytes 600064 | tf_op jit(solution)/shard_map/convert_element_type | solution.py:70
  6.6 0.5 fusion.54
  7.8 1.3 %reshape.155 = bf16[4,2,9216]{2,1,0:T(2,128)(2,1)} reshape(bf16[64,24,48]{2,1,0:T(8,128)(2,1)S(1)} %copy.63) | data formatting | bytes 294912
  9.0 6.3 %all-to-all-start.1 = ((bf16[4,2,9216]{2,1,0:T(2,128)(2,1)}), bf16[4,2,9216]{2,1,0:T(2,128)(2,1)S(1)}, u32[]{:S(2)}, u32[]{:S(2)}) async-start(bf16[4,2,9216]{2,1,0:T(2,128)(2,1)} %reshape.155), calls=%async_computation.1 | async-start | bytes 294912 | tf_op jit(solution)/shard_map/all_to_all | solution.py:75
  15.6 1.2 %reshape.159 = bf16[4,2,9216]{2,1,0:T(2,128)(2,1)} reshape(bf16[64,24,48]{2,1,0:T(8,128)(2,1)S(1)} %copy.60) | data formatting | bytes 294912
  16.9 4.7 %all-to-all-done.1 = bf16[4,2,9216]{2,1,0:T(2,128)(2,1)S(1)} async-done(((bf16[4,2,9216]{2,1,0:T(2,128)(2,1)}), bf16[4,2,9216]{2,1,0:T(2,128)(2,1)S(1)}, u32[]{:S(2)}, u32[]{:S(2)}) %all-to-all-start.1) | async-done | bytes 147488 | tf_op jit(solution)/shard_map/all_to_all | solution.py:75
  21.6 3.3 %all-to-all-start = ((bf16[4,2,9216]{2,1,0:T(2,128)(2,1)}), bf16[4,2,9216]{2,1,0:T(2,128)(2,1)S(1)}, u32[]{:S(2)}, u32[]{:S(2)}) async-start(bf16[4,2,9216]{2,1,0:T(2,128)(2,1)} %reshape.159), calls=%async_computation | async-start | bytes 294912 | tf_op jit(solution)/shard_map/all_to_all | solution.py:74
  25.8 1.2 %reshape.157 = bf16[2,2,18432]{2,1,0:T(2,128)(2,1)} reshape(bf16[96,16,48]{2,1,0:T(8,128)(2,1)S(1)} %bitcast.191) | data formatting | bytes 294912
  27.1 3.8 %all-to-all-done = bf16[4,2,9216]{2,1,0:T(2,128)(2,1)S(1)} async-done(((bf16[4,2,9216]{2,1,0:T(2,128)(2,1)}), bf16[4,2,9216]{2,1,0:T(2,128)(2,1)S(1)}, u32[]{:S(2)}, u32[]{:S(2)}) %all-to-all-start) | async-done | bytes 147488 | tf_op jit(solution)/shard_map/all_to_all | solution.py:74
  30.9 3.4 %all-to-all-start.2 = ((bf16[2,2,18432]{2,1,0:T(2,128)(2,1)}), bf16[2,2,18432]{2,1,0:T(2,128)(2,1)S(1)}, u32[]{:S(2)}, u32[]{:S(2)}) async-start(bf16[2,2,18432]{2,1,0:T(2,128)(2,1)} %reshape.157), calls=%async_computation.2 | async-start | bytes 294912 | tf_op jit(solution)/shard_map/all_to_all | solution.py:30
  34.9 6.5 %all_gather.9 = bf16[16,96,96]{1,2,0:T(8,128)(2,1)S(1)} all-gather(bf16[16,96,48]{1,2,0:T(8,128)(2,1)S(1)} %copy.62), channel_id=1, replica_groups=mesh['groups'=2,'row'=4,'col'=2,'chan'=2] {'col'}, dimensions={2}, use_global_device_ids=true | all-gather | bytes 442368 | tf_op jit(solution)/shard_map/all_gather | solution.py:24
  43.0 1.3 %reshape.161 = bf16[4,2,9216]{2,1,0:T(2,128)(2,1)} reshape(bf16[96,16,48]{2,1,0:T(8,128)(2,1)S(1)} %bitcast.196) | data formatting | bytes 294912
  44.3 3.3 %all-to-all-start.3 = ((bf16[4,2,9216]{2,1,0:T(2,128)(2,1)}), bf16[4,2,9216]{2,1,0:T(2,128)(2,1)S(1)}, u32[]{:S(2)}, u32[]{:S(2)}) async-start(bf16[4,2,9216]{2,1,0:T(2,128)(2,1)} %reshape.161), calls=%async_computation.3 | async-start | bytes 294912 | tf_op jit(solution)/shard_map/all_to_all | solution.py:78
  47.9 5.7 %all-to-all-done.3 = bf16[4,2,9216]{2,1,0:T(2,128)(2,1)S(1)} async-done(((bf16[4,2,9216]{2,1,0:T(2,128)(2,1)}), bf16[4,2,9216]{2,1,0:T(2,128)(2,1)S(1)}, u32[]{:S(2)}, u32[]{:S(2)}) %all-to-all-start.3) | async-done | bytes 147488 | tf_op jit(solution)/shard_map/all_to_all | solution.py:78
  54.6 3.8 %all_to_all.144 = bf16[2,2,18432]{2,1,0:T(2,128)(2,1)S(1)} all-to-all(bf16[2,2,18432]{2,1,0:T(2,128)(2,1)S(1)} %reshape.163), channel_id=1, replica_groups=mesh['groups'=2,'row'=4,'col'=2,'chan'=2] {'chan'}, dimensions={0} | all-to-all | bytes 294912 | tf_op jit(solution)/shard_map/all_to_all | solution.py:79
  60.1 2.4 %all_gather.10 = f32[24,48,128]{2,1,0:T(8,128)S(1)} all-gather(f32[12,48,128]{2,1,0:T(8,128)S(1)} %fusion.1), channel_id=1, replica_groups=mesh['groups'=2,'row'=4,'col'=2,'chan'=2] {'chan'}, dimensions={0}, use_global_device_ids=true | all-gather | bytes 884736 | tf_op jit(solution)/shard_map/all_gather | solution.py:69
  64.7 1.3 %reshape.165 = bf16[4,2,9216]{2,1,0:T(2,128)(2,1)} reshape(bf16[64,24,48]{2,1,0:T(8,128)(2,1)S(1)} %copy.74) | data formatting | bytes 294912
  66.0 3.3 %all-to-all-start.5 = ((bf16[4,2,9216]{2,1,0:T(2,128)(2,1)}), bf16[4,2,9216]{2,1,0:T(2,128)(2,1)S(1)}, u32[]{:S(2)}, u32[]{:S(2)}) async-start(bf16[4,2,9216]{2,1,0:T(2,128)(2,1)} %reshape.165), calls=%async_computation.5 | async-start | bytes 294912 | tf_op jit(solution)/shard_map/all_to_all | solution.py:74
  69.6 1.2 %reshape.167 = bf16[4,2,9216]{2,1,0:T(2,128)(2,1)} reshape(bf16[64,24,48]{2,1,0:T(8,128)(2,1)S(1)} %copy.77) | data formatting | bytes 294912
  70.8 5.1 %all-to-all-done.5 = bf16[4,2,9216]{2,1,0:T(2,128)(2,1)S(1)} async-done(((bf16[4,2,9216]{2,1,0:T(2,128)(2,1)}), bf16[4,2,9216]{2,1,0:T(2,128)(2,1)S(1)}, u32[]{:S(2)}, u32[]{:S(2)}) %all-to-all-start.5) | async-done | bytes 147488 | tf_op jit(solution)/shard_map/all_to_all | solution.py:74
  75.9 3.3 %all-to-all-start.6 = ((bf16[4,2,9216]{2,1,0:T(2,128)(2,1)}), bf16[4,2,9216]{2,1,0:T(2,128)(2,1)S(1)}, u32[]{:S(2)}, u32[]{:S(2)}) async-start(bf16[4,2,9216]{2,1,0:T(2,128)(2,1)} %reshape.167), calls=%async_computation.6 | async-start | bytes 294912 | tf_op jit(solution)/shard_map/all_to_all | solution.py:75
  80.0 6.6 %all_gather.11 = bf16[16,96,96]{1,2,0:T(8,128)(2,1)S(1)} all-gather(bf16[16,96,48]{1,2,0:T(8,128)(2,1)S(1)} %copy.76), channel_id=1, replica_groups=mesh['groups'=2,'row'=4,'col'=2,'chan'=2] {'col'}, dimensions={2}, use_global_device_ids=true | all-gather | bytes 442368 | tf_op jit(solution)/shard_map/all_gather | solution.py:24
  87.8 1.3 %reshape.169 = bf16[4,2,9216]{2,1,0:T(2,128)(2,1)} reshape(bf16[96,16,48]{2,1,0:T(8,128)(2,1)S(1)} %bitcast.201) | data formatting | bytes 294912
  89.1 4.8 %all-to-all-start.7 = ((bf16[4,2,9216]{2,1,0:T(2,128)(2,1)}), bf16[4,2,9216]{2,1,0:T(2,128)(2,1)S(1)}, u32[]{:S(2)}, u32[]{:S(2)}) async-start(bf16[4,2,9216]{2,1,0:T(2,128)(2,1)} %reshape.169), calls=%async_computation.7 | async-start | bytes 294912 | tf_op jit(solution)/shard_map/all_to_all | solution.py:78
  94.1 5.7 %all-to-all-done.7 = bf16[4,2,9216]{2,1,0:T(2,128)(2,1)S(1)} async-done(((bf16[4,2,9216]{2,1,0:T(2,128)(2,1)}), bf16[4,2,9216]{2,1,0:T(2,128)(2,1)S(1)}, u32[]{:S(2)}, u32[]{:S(2)}) %all-to-all-start.7) | async-done | bytes 147488 | tf_op jit(solution)/shard_map/all_to_all | solution.py:78
  100.9 3.8 %all_to_all.145 = bf16[2,2,18432]{2,1,0:T(2,128)(2,1)S(1)} all-to-all(bf16[2,2,18432]{2,1,0:T(2,128)(2,1)S(1)} %reshape.171), channel_id=1, replica_groups=mesh['groups'=2,'row'=4,'col'=2,'chan'=2] {'chan'}, dimensions={0} | all-to-all | bytes 294912 | tf_op jit(solution)/shard_map/all_to_all | solution.py:79
  106.1 0.9 fusion
  (80 shorter events, 13.8 us)
Async XLA Ops:
  7.1 17.8 %copy-start = (bf16[24,48,128]{2,1,0:T(8,128)(2,1)S(1)}, bf16[24,48,128]{2,1,0:T(8,128)(2,1)}, u32[]{:S(2)}) copy-start(bf16[24,48,128]{2,1,0:T(8,128)(2,1)} %param.9) | copy-start | bytes 884740
  7.5 17.5 %copy-start.2 = (f32[2,128]{1,0:T(2,128)S(1)}, f32[2,128]{1,0:T(2,128)}, u32[]{:S(2)}) copy-start(f32[2,128]{1,0:T(2,128)} %param.16) | copy-start | bytes 3076
  7.5 17.5 %copy-start.3 = (f32[2,128]{1,0:T(2,128)S(1)}, f32[2,128]{1,0:T(2,128)}, u32[]{:S(2)}) copy-start(f32[2,128]{1,0:T(2,128)} %param.15) | copy-start | bytes 3076
  9.0 12.6 %all-to-all-start.1 = ((bf16[4,2,9216]{2,1,0:T(2,128)(2,1)}), bf16[4,2,9216]{2,1,0:T(2,128)(2,1)S(1)}, u32[]{:S(2)}, u32[]{:S(2)}) async-start(bf16[4,2,9216]{2,1,0:T(2,128)(2,1)} %reshape.155), calls=%async_computation.1 | async-start | bytes 294912 | tf_op jit(solution)/shard_map/all_to_all | solution.py:75
  21.6 9.3 %all-to-all-start = ((bf16[4,2,9216]{2,1,0:T(2,128)(2,1)}), bf16[4,2,9216]{2,1,0:T(2,128)(2,1)S(1)}, u32[]{:S(2)}, u32[]{:S(2)}) async-start(bf16[4,2,9216]{2,1,0:T(2,128)(2,1)} %reshape.159), calls=%async_computation | async-start | bytes 294912 | tf_op jit(solution)/shard_map/all_to_all | solution.py:74
  30.9 10.5 %all-to-all-start.2 = ((bf16[2,2,18432]{2,1,0:T(2,128)(2,1)}), bf16[2,2,18432]{2,1,0:T(2,128)(2,1)S(1)}, u32[]{:S(2)}, u32[]{:S(2)}) async-start(bf16[2,2,18432]{2,1,0:T(2,128)(2,1)} %reshape.157), calls=%async_computation.2 | async-start | bytes 294912 | tf_op jit(solution)/shard_map/all_to_all | solution.py:30
  34.9 12.7 %copy-start.4 = (bf16[2,128,128]{2,1,0:T(8,128)(2,1)S(1)}, bf16[2,128,128]{2,1,0:T(8,128)(2,1)}, u32[]{:S(2)}) copy-start(bf16[2,128,128]{2,1,0:T(8,128)(2,1)} %param.14) | copy-start | bytes 196612
  44.3 9.3 %all-to-all-start.3 = ((bf16[4,2,9216]{2,1,0:T(2,128)(2,1)}), bf16[4,2,9216]{2,1,0:T(2,128)(2,1)S(1)}, u32[]{:S(2)}, u32[]{:S(2)}) async-start(bf16[4,2,9216]{2,1,0:T(2,128)(2,1)} %reshape.161), calls=%async_computation.3 | async-start | bytes 294912 | tf_op jit(solution)/shard_map/all_to_all | solution.py:78
  53.9 5.9 %copy-start.1 = (bf16[2,128,128]{2,1,0:T(8,128)(2,1)S(1)}, bf16[2,128,128]{2,1,0:T(8,128)(2,1)}, u32[]{:S(2)}) copy-start(bf16[2,128,128]{2,1,0:T(8,128)(2,1)} %param.17) | copy-start | bytes 196612
  66.0 10.0 %all-to-all-start.5 = ((bf16[4,2,9216]{2,1,0:T(2,128)(2,1)}), bf16[4,2,9216]{2,1,0:T(2,128)(2,1)S(1)}, u32[]{:S(2)}, u32[]{:S(2)}) async-start(bf16[4,2,9216]{2,1,0:T(2,128)(2,1)} %reshape.165), calls=%async_computation.5 | async-start | bytes 294912 | tf_op jit(solution)/shard_map/all_to_all | solution.py:74
  75.9 10.7 %all-to-all-start.6 = ((bf16[4,2,9216]{2,1,0:T(2,128)(2,1)}), bf16[4,2,9216]{2,1,0:T(2,128)(2,1)S(1)}, u32[]{:S(2)}, u32[]{:S(2)}) async-start(bf16[4,2,9216]{2,1,0:T(2,128)(2,1)} %reshape.167), calls=%async_computation.6 | async-start | bytes 294912 | tf_op jit(solution)/shard_map/all_to_all | solution.py:75
  89.1 10.8 %all-to-all-start.7 = ((bf16[4,2,9216]{2,1,0:T(2,128)(2,1)}), bf16[4,2,9216]{2,1,0:T(2,128)(2,1)S(1)}, u32[]{:S(2)}, u32[]{:S(2)}) async-start(bf16[4,2,9216]{2,1,0:T(2,128)(2,1)} %reshape.169), calls=%async_computation.7 | async-start | bytes 294912 | tf_op jit(solution)/shard_map/all_to_all | solution.py:78
where the time goes:
time: 108 us; the launch traced here: 107 us
  starting transfers between devices  27.9 us (26%)
  waiting for transfers between devices  25.1 us (23%)
  blocking collectives  23.2 us (21%)
  local copies, waits for them, and re-layouts  19.3 us (18%)
  other arithmetic  7.79 us (7%)
  matrix products  3.21 us (3%)
    all_gather x2, blocking collectives, triangle_core(): full_left = lax.all_gather(left_side, 'col', axis=2, tiled=True)  13.1 us
    unnamed x28, local copies, waits for them, and re-layouts  12.4 us
    all_to_all x2, waiting for transfers between devices, local(): lax.all_to_all(product, 'row', split_axis=1, concat_axis=0, tiled=True)  11.4 us
    all_to_all x2, starting transfers between devices, local(): lax.all_to_all(right_side, 'row', split_axis=0, concat_axis=1, tiled=True)  9.65 us
    all_to_all x2, waiting for transfers between devices, local(): lax.all_to_all(left_side, 'row', split_axis=0, concat_axis=1, tiled=True)  8.92 us
    all_to_all x2, starting transfers between devices, local(): lax.all_to_all(product, 'row', split_axis=1, concat_axis=0, tiled=True)  8.15 us
    all_to_all x2, blocking collectives, local(): lax.all_to_all(returned, 'chan', split_axis=1, concat_axis=0, tiled=True)  7.65 us
    all_to_all x2, starting transfers between devices, local(): lax.all_to_all(left_side, 'row', split_axis=0, concat_axis=1, tiled=True)  6.67 us
  transfers between devices with their start and end apart: 7, of which 5 were waited for; matrix products, arithmetic and copies ran while one was open for 6% of the time, Pallas kernels for 0%

commit v1 on v0

--- a/solution.py
+++ b/solution.py
@@ -1,6 +1,10 @@
+import functools
+
 import jax
 import jax.numpy as jnp
 from jax import lax
+from jax.experimental import pallas as pl
+from jax.experimental.pallas import tpu as pltpu
 from jax.sharding import PartitionSpec as P
 
 EPSILON = 1e-05
@@ -85,7 +89,365 @@
     return pair_now
 
 
+MESH = pl.DeviceIdType.MESH
+
+
+def fused_norm(values, gain_vec, offset):
+    average = jnp.mean(values, axis=-1, keepdims=True)
+    centred = values - average
+    variance = jnp.mean(centred * centred, axis=-1, keepdims=True)
+    return (centred * lax.rsqrt(variance + EPSILON) * gain_vec + offset).astype(jnp.bfloat16)
+
+
+def dot_f32(a, b):
+    return jnp.dot(a, b, preferred_element_type=jnp.float32)
+
+
+def fused_kernel(
+    sizes, pair_ref, mask_rows_ref, mask_cols_ref, in_gain_ref, in_bias_ref, w_proj_ref, w_gate_ref,
+    out_gain_ref, out_bias_ref, w_out_ref, out_ref,
+    right_all, left_f32, right_f32, part_f32, part_send, part_recv, left_cut, left_send, left_all,
+    left_blk, tri, pair_1, gate,
+    right_recv_sem, right_fwd_sem, right_sib_sem, part_send_sem, part_recv_sem, left_send_sem, left_recv_sem,
+):
+    rows, cols, cores, half, width = sizes
+    blocks = rows * cores
+    per_col = blocks // cols
+    tokens = half * width
+    cell = half * half
+    z = lax.axis_index("row")
+    x = lax.axis_index("col")
+    c = lax.axis_index("chan")
+    me = z * cores + c
+    sib = 1 - c
+    channels = pair_ref.shape[-1]
+
+    barrier = pltpu.get_barrier_semaphore()
+    for dz in range(rows):
+        for dx in range(cols):
+            for dc in range(cores):
+                if dz or dx or dc:
+                    pl.semaphore_signal(
+                        barrier, inc=1,
+                        device_id={
+                            "row": lax.rem(z + dz, rows),
+                            "col": lax.rem(x + dx, cols),
+                            "chan": lax.rem(c + dc, cores),
+                        },
+                        device_id_type=MESH,
+                    )
+
+    def right_copy(layer, zb, cb, send_sem, device_id):
+        return pltpu.make_async_remote_copy(
+            src_ref=right_all.at[layer, zb, cb],
+            dst_ref=right_all.at[layer, zb, cb],
+            send_sem=send_sem,
+            recv_sem=right_recv_sem.at[layer, zb, cb],
+            device_id=device_id,
+            device_id_type=MESH,
+        )
+
+    def fwd_right(layer, zb):
+        return right_copy(layer, zb, c, right_fwd_sem.at[layer, zb], {"row": z + 1})
+
+    def fwd_left(layer, zb, slot):
+        return right_copy(layer, zb, c, right_fwd_sem.at[layer, slot], {"row": z - 1})
+
+    def to_sib(layer, zb):
+        return right_copy(layer, zb, c, right_sib_sem.at[layer, zb], {"chan": sib})
+
+    def start_right(layer):
+        @pl.when(z + 1 < rows)
+        def _():
+            fwd_right(layer, z).start()
+
+        @pl.when(z > 0)
+        def _():
+            fwd_left(layer, z, rows).start()
+
+        to_sib(layer, z).start()
+
+    def relay(layer, s):
+        @pl.when(z - s >= 0)
+        def _():
+            right_copy(layer, z - s, c, right_sib_sem.at[layer, z - s], {"chan": sib}).wait_recv()
+
+            @pl.when(z + 1 < rows)
+            def _():
+                fwd_right(layer, z - s).start()
+
+            to_sib(layer, z - s).start()
+
+        @pl.when(z + s < rows)
+        def _():
+            right_copy(layer, z + s, c, right_sib_sem.at[layer, z + s], {"chan": sib}).wait_recv()
+
+            @pl.when(z > 0)
+            def _():
+                fwd_left(layer, z + s, z + s).start()
+
+            to_sib(layer, z + s).start()
+
+    def finish_right(layer):
+        @pl.when(z + 1 < rows)
+        def _():
+            fwd_right(layer, z).wait_send()
+
+        @pl.when(z > 0)
+        def _():
+            fwd_left(layer, z, rows).wait_send()
+
+        to_sib(layer, z).wait_send()
+        for s in range(1, rows):
+            @pl.when(z - s >= 0)
+            def _():
+                @pl.when(z + 1 < rows)
+                def _():
+                    fwd_right(layer, z - s).wait_send()
+
+                to_sib(layer, z - s).wait_send()
+
+            @pl.when(z + s < rows)
+            def _():
+                @pl.when(z > 0)
+                def _():
+                    fwd_left(layer, z + s, z + s).wait_send()
+
+                to_sib(layer, z + s).wait_send()
+
+    def each_block(layer, work):
+        work(z, c)
+        right_copy(layer, z, sib, right_sib_sem.at[layer, z], {"chan": sib}).wait_recv()
+        work(z, sib)
+
+        def at_distance(s, _):
+            relay(layer, s)
+
+            def one(t, _):
+                zb = z + s * (2 * (t % 2) - 1)
+                cb = (c + t // 2) % 2
+
+                @pl.when((zb >= 0) & (zb < rows))
+                def _():
+                    @pl.when(t >= 2)
+                    def _():
+                        right_copy(layer, zb, cb, right_sib_sem.at[layer, zb], {"chan": sib}).wait_recv()
+
+                    work(zb, cb)
+
+                return 0
+
+            lax.fori_loop(0, 4, one, 0)
+            return 0
+
+        lax.fori_loop(1, rows, at_distance, 0)
+
+    mask_cols = mask_cols_ref[pl.ds(pl.multiple_of(x * width, 8), width)]
+    mask_tile = mask_rows_ref[pl.ds(me * half, half)] * mask_cols[None]
+
+    def gated(normed, layer, which):
+        opened = jax.nn.sigmoid(dot_f32(normed, w_proj_ref[layer, which]))
+        value = opened * dot_f32(normed, w_proj_ref[layer, which + 1])
+        return (mask_tile * value.reshape(half, width, channels)).astype(jnp.bfloat16)
+
+    def finish_layer_here(layer, pair_now):
+        unit = fused_norm(
+            tri[...].reshape(tokens, channels).astype(jnp.bfloat16).astype(jnp.float32),
+            out_gain_ref[pl.ds(layer, 1)], out_bias_ref[pl.ds(layer, 1)],
+        )
+        return pair_now + gate[...] * dot_f32(unit, w_out_ref[layer])
+
+    pair_0 = pair_ref[pl.ds(c * half, half)].astype(jnp.float32).reshape(tokens, channels)
+    normed = fused_norm(pair_0, in_gain_ref[pl.ds(0, 1)], in_bias_ref[pl.ds(0, 1)])
+    right_all[0, z, c] = gated(normed, 0, 2)
+    pl.semaphore_wait(barrier, blocks * cols - 1)
+    start_right(0)
+    left_f32[...] = gated(normed, 0, 0).astype(jnp.float32)
+    gate[...] = jax.nn.sigmoid(dot_f32(normed, w_gate_ref[0]))
+
+    def part_copy(q, dx, zb_cb):
+        return pltpu.make_async_remote_copy(
+            src_ref=part_send.at[zb_cb],
+            dst_ref=part_recv.at[x, q],
+            send_sem=part_send_sem.at[zb_cb],
+            recv_sem=part_recv_sem.at[x, q],
+            device_id={"col": dx},
+            device_id_type=MESH,
+        )
+
+    def outgoing(zb, cb):
+        b = zb * cores + cb
+        right_f32[...] = right_all[0, zb, cb].astype(jnp.float32)
+
+        def one_row(i, _):
+            left_row = left_f32[i]
+            left_blk[i] = jnp.sum(left_row[None] * right_f32[...], axis=1)
+            return 0
+
+        lax.fori_loop(0, half, one_row, 0)
+        for i in range(half):
+            part_f32[b, i * half:(i + 1) * half] = left_blk[i]
+
+        @pl.when(b // per_col != x)
+        def _():
+            part_send[b] = part_f32[b].astype(jnp.bfloat16)
+            part_copy(b % per_col, b // per_col, b).start()
+
+    each_block(0, outgoing)
+
+    for q in range(per_col):
+        total = part_f32[x * per_col + q]
+        for d in range(1, cols):
+            xs = lax.rem(x + d, cols)
+            pltpu.make_async_remote_copy(
+                src_ref=part_send.at[0], dst_ref=part_recv.at[xs, q],
+                send_sem=part_send_sem.at[0], recv_sem=part_recv_sem.at[xs, q],
+                device_id={"col": xs}, device_id_type=MESH,
+            ).wait_recv()
+            total = total + part_recv[xs, q].astype(jnp.float32)
+        for i in range(half):
+            tri[i, q * half:(q + 1) * half] = total[i * half:(i + 1) * half]
+
+    pair_1[...] = finish_layer_here(0, pair_0)
+
+    normed = fused_norm(pair_1[...], in_gain_ref[pl.ds(1, 1)], in_bias_ref[pl.ds(1, 1)])
+    right_all[1, z, c] = gated(normed, 1, 2)
+    start_right(1)
+    left_f32[...] = gated(normed, 1, 0).astype(jnp.float32)
+    for p in range(per_col):
+        for k in range(half):
+            left_cut[p, k * half:(k + 1) * half] = left_f32[k, p * half:(p + 1) * half]
+        left_send[p] = left_cut[p].astype(jnp.bfloat16)
+
+    def left_copy(p, dx):
+        b = x * per_col + p
+        return pltpu.make_async_remote_copy(
+            src_ref=left_send.at[p],
+            dst_ref=left_all.at[me],
+            send_sem=left_send_sem.at[p, dx],
+            recv_sem=left_recv_sem.at[me],
+            device_id={"row": b // cores, "col": dx, "chan": b % cores},
+            device_id_type=MESH,
+        )
+
+    for p in range(per_col):
+        for dx in range(cols):
+            is_me = (x * per_col + p == me) & (x == dx)
+
+            @pl.when(jnp.logical_not(is_me))
+            def _():
+                left_copy(p, dx).start()
+
+            @pl.when(is_me)
+            def _():
+                left_all[me] = left_send[p]
+
+    gate[...] = jax.nn.sigmoid(dot_f32(normed, w_gate_ref[1]))
+    tri[...] = jnp.zeros_like(tri)
+    step = 4 if half % 4 == 0 else 1
+
+    def incoming(zb, cb):
+        b = zb * cores + cb
+
+        @pl.when(jnp.logical_not((b == me) & (x == me // per_col)))
+        def _():
+            pltpu.make_async_remote_copy(
+                src_ref=left_send.at[0], dst_ref=left_all.at[b],
+                send_sem=left_send_sem.at[0, 0], recv_sem=left_recv_sem.at[b],
+                device_id={"chan": sib}, device_id_type=MESH,
+            ).wait_recv()
+
+        left_cut[0] = left_all[b].astype(jnp.float32)
+        right_f32[...] = right_all[1, zb, cb].astype(jnp.float32)
+        for i0 in range(0, half, step):
+            sums = [tri[i0 + i] for i in range(step)]
+            for k in range(half):
+                right_row = right_f32[k]
+                for i in range(step):
+                    at = k * half + i0 + i
+                    sums[i] = sums[i] + left_cut[0, at:at + 1] * right_row
+            for i in range(step):
+                tri[i0 + i] = sums[i]
+
+    each_block(1, incoming)
+    out_ref[...] = finish_layer_here(1, pair_1[...]).reshape(half, width, channels)
+
+    finish_right(0)
+    finish_right(1)
+    for b in range(blocks):
+        @pl.when(b // per_col != x)
+        def _():
+            part_copy(b % per_col, b // per_col, b).wait_send()
+
+    for p in range(per_col):
+        for dx in range(cols):
+            @pl.when(jnp.logical_not((x * per_col + p == me) & (x == dx)))
+            def _():
+                left_copy(p, dx).wait_send()
+
+
+def fused_local(
+    sizes, pair_act, res_mask, in_gain, in_bias, w_proj, w_gate, out_gain, out_bias, w_out
+):
+    rows, cols, cores, half, width = sizes
+    blocks = rows * cores
+    per_col = blocks // cols
+    cell = half * half
+    channels = pair_act.shape[-1]
+    mask_cols = jnp.broadcast_to(res_mask.astype(jnp.float32)[:, None], (res_mask.shape[0], channels))
+    mask_rows = mask_cols[:, None, :]
+    f32, bf16, dma = jnp.float32, jnp.bfloat16, pltpu.SemaphoreType.DMA
+    return pl.pallas_call(
+        functools.partial(fused_kernel, sizes),
+        out_shape=jax.ShapeDtypeStruct((half, width, channels), f32),
+        in_specs=[pl.BlockSpec(memory_space=pltpu.VMEM)] * 10,
+        out_specs=pl.BlockSpec(memory_space=pltpu.VMEM),
+        scratch_shapes=[
+            pltpu.VMEM((2, rows, cores, half, width, channels), bf16),
+            pltpu.VMEM((half, width, channels), f32),
+            pltpu.VMEM((half, width, channels), f32),
+            pltpu.VMEM((blocks, cell, channels), f32),
+            pltpu.VMEM((blocks, cell, channels), bf16),
+            pltpu.VMEM((cols, per_col, cell, channels), bf16),
+            pltpu.VMEM((per_col, cell, channels), f32),
+            pltpu.VMEM((per_col, cell, channels), bf16),
+            pltpu.VMEM((blocks, cell, channels), bf16),
+            pltpu.VMEM((half, half, channels), f32),
+            pltpu.VMEM((half, width, channels), f32),
+            pltpu.VMEM((half * width, channels), f32),
+            pltpu.VMEM((half * width, channels), f32),
+            dma((2, rows, cores)),
+            dma((2, rows + 1)),
+            dma((2, rows)),
+            dma((blocks,)),
+            dma((cols, per_col)),
+            dma((per_col, cols)),
+            dma((blocks,)),
+        ],
+        compiler_params=pltpu.CompilerParams(
+            collective_id=0, has_side_effects=True, vmem_limit_bytes=48 * 1024 * 1024
+        ),
+    )(pair_act, mask_rows, mask_cols, in_gain, in_bias, w_proj, w_gate, out_gain, out_bias, w_out)
+
+
+def local_any(
+    axis_sizes, pair_act, res_mask, in_gain, in_bias, w_proj, w_gate, out_gain, out_bias, w_out
+):
+    rows, cols, cores = axis_sizes
+    half = pair_act.shape[0] // cores
+    width = pair_act.shape[1]
+    blocks = rows * cores
+    fits = cores == 2 and blocks % cols == 0 and width == half * (blocks // cols)
+    fits = fits and width % 16 == 0 and (half * half) % 16 == 0
+    fits = fits and blocks * half * width * pair_act.shape[2] <= 1 << 20
+    args = (pair_act, res_mask, in_gain, in_bias, w_proj, w_gate, out_gain, out_bias, w_out)
+    if fits:
+        return fused_local((rows, cols, cores, half, width), *args)
+    return local(*args)
+
+
 def solution(mesh):
+    axis_sizes = tuple(mesh.shape[name] for name in ("row", "col", "chan"))
     in_specs = (P(("groups", "row"), "col", None), P("groups"), P(), P(), P(), P(), P(), P(), P())
     out_specs = P(("groups", "row", "chan"), "col", None)
-    return jax.shard_map(local, mesh=mesh, in_specs=in_specs, out_specs=out_specs, check_vma=False)
+    return jax.shard_map(functools.partial(local_any, axis_sizes), mesh=mesh, in_specs=in_specs, out_specs=out_specs, check_vma=False)

time: 108 us -> 53.5 us (0.50)
  Pallas kernels: 0 us -> 47.7 us
  starting transfers between devices: 27.9 us -> 0 us
  waiting for transfers between devices: 25.1 us -> 0 us
  blocking collectives: 23.2 us -> 0 us
  local copies, waits for them, and re-layouts: 19.3 us -> 4.24 us
  other arithmetic: 7.79 us -> 0.69 us
  matrix products: 3.21 us -> 0 us
    pallas_call x0 -> x1, Pallas kernels: none -> 47.7 us  [fused_local(): pl.pallas_call(functools.partial(fused_kernel, sizes), out_shape=jax.Shap...]
    all_to_all x7 -> x0, starting transfers between devices: 27.9 us -> none  [the longest x2 9.65 us: local(): lax.all_to_all(right_side, 'row', split_axis=0, concat_axis=1, tiled=True)]
    all_to_all x7 -> x0, waiting for transfers between devices: 25.1 us -> none  [the longest x2 11.4 us: local(): lax.all_to_all(product, 'row', split_axis=1, concat_axis=0, tiled=True)]
    all_gather x3 -> x0, blocking collectives: 15.5 us -> none  [the longest x2 13.1 us: triangle_core(): full_left = lax.all_gather(left_side, 'col', axis=2, tiled=True)]
    unnamed x28 -> x17, local copies, waits for them, and re-layouts: 12.4 us -> 4.01 us
    all_to_all x2 -> x0, blocking collectives: 7.65 us -> none  [local(): lax.all_to_all(returned, 'chan', split_axis=1, concat_axis=0, tiled=True)]
    reduce_sum x8 -> x0, other arithmetic: 4.11 us -> none  [the longest x4 2.39 us: layer_norm(): variance = jnp.mean(centred * centred, axis=norm_axis, keepdims=True)]
    dot_general x8 -> x0, matrix products: 3.21 us -> none  [the longest x2 1.08 us: finish_layer(): jnp.einsum('ers,ez->rsz', unit_act, w_out_layer, preferred_element_type=j...]
  transfers between devices with their start and end apart: 7 -> 0, of which waited for: 5 -> 0; matrix products, arithmetic and copies ran while one was open for 6% -> 0% of each run, Pallas kernels for 0% -> 0%
where the time goes in v1:
time: 53.5 us; the launch traced here: 52.7 us
  Pallas kernels  47.7 us (89%)
  local copies, waits for them, and re-layouts  4.24 us (8%)
  other arithmetic  0.69 us (1%)
    pallas_call x1, Pallas kernels, fused_local(): pl.pallas_call(functools.partial(fused_kernel, sizes), out_shape=jax.Shap...  47.7 us
    unnamed x17, local copies, waits for them, and re-layouts  4.01 us

profile of v1, /device:TPU:0, one launch (start us, length us, event | category | flops | bytes accessed | tf_op | source)
XLA Modules:
  0.0 52.7 jit_solution(14701881147894801078)
XLA Ops:
  0.0 0.0 copy-start.2
  0.0 0.7 %convert_element_type.3 = f32[96]{0:T(128)S(1)} convert(s32[96]{0:T(128)} %param.10) | non-fusion elementwise | flops 96 | bytes 768 | tf_op jit(solution)/shard_map/convert_element_type | solution.py:397
  0.7 0.1 broadcast_in_dim.2.mask_cols_ref
  0.8 0.0 copy-start.4
  0.8 0.0 copy-start.5
  0.8 0.0 copy-start.6
  0.8 0.0 copy-start.7
  0.8 0.2 broadcast_in_dim_broadcast_in_dim.2.mask_rows_ref
  1.0 0.0 copy-done.2
  1.0 0.5 copy-done.4
  1.5 0.0 copy-done.5
  1.5 0.0 copy-done.6
  1.5 0.0 copy-done.7
  1.5 0.0 copy-start
  1.5 1.0 %copy-done = bf16[24,48,128]{2,1,0:T(8,128)(2,1)S(1)} copy-done((bf16[24,48,128]{2,1,0:T(8,128)(2,1)S(1)}, bf16[24,48,128]{2,1,0:T(8,128)(2,1)}, u32[]{:S(2)}) %copy-start) | copy-done | bytes 294936
  2.5 0.0 copy-start.1
  2.5 0.9 %copy-done.1 = bf16[2,4,128,128]{3,2,1,0:T(8,128)(2,1)S(1)} copy-done((bf16[2,4,128,128]{3,2,1,0:T(8,128)(2,1)S(1)}, bf16[2,4,128,128]{3,2,1,0:T(8,128)(2,1)}, u32[]{:S(2)}) %copy-start.1) | copy-done | bytes 262168
  3.4 0.0 copy-start.3
  3.4 0.8 %copy-done.3 = bf16[2,128,128]{2,1,0:T(8,128)(2,1)S(1)} copy-done((bf16[2,128,128]{2,1,0:T(8,128)(2,1)S(1)}, bf16[2,128,128]{2,1,0:T(8,128)(2,1)}, u32[]{:S(2)}) %copy-start.3) | copy-done | bytes 65560
  4.3 47.7 %shard_map.91 = f32[12,48,128]{2,1,0:T(8,128)S(1)} custom-call(bf16[24,48,128]{2,1,0:T(8,128)(2,1)S(1)} %copy-done, f32[96,1,128]{2,1,0:T(1,128)S(1)} %broadcast_in_dim_broadcast_in_dim.2.mask_rows_ref, f32[96,128]{1,0:T(8,128)S(1)} %broadcast_in_dim.2.mask_cols_ref, f32[2,128]{1,0:T(2,128)S(1)} %copy-done.4, f32[2,128]{1,0:T(2,128)S(1)} %copy-done.5, ...), custom_call_target="tpu_custom_call" | custom-call | tf_op jit(solution)/shard_map/pallas_call | solution.py:400
  51.9 0.7 %copy.11 = f32[12,48,128]{2,1,0:T(8,128)} copy(f32[12,48,128]{2,1,0:T(8,128)S(1)} %shard_map.91) | data formatting | bytes 589824
Async XLA Ops:
  0.0 1.0 %copy-start.2 = (bf16[2,128,128]{2,1,0:T(8,128)(2,1)S(1)}, bf16[2,128,128]{2,1,0:T(8,128)(2,1)}, u32[]{:S(2)}) copy-start(bf16[2,128,128]{2,1,0:T(8,128)(2,1)} %w_gate_ref.1) | copy-start | bytes 196612
  0.8 0.7 %copy-start.4 = (f32[2,128]{1,0:T(2,128)S(1)}, f32[2,128]{1,0:T(2,128)}, u32[]{:S(2)}) copy-start(f32[2,128]{1,0:T(2,128)} %in_gain_ref.1) | copy-start | bytes 3076
  0.8 0.7 %copy-start.5 = (f32[2,128]{1,0:T(2,128)S(1)}, f32[2,128]{1,0:T(2,128)}, u32[]{:S(2)}) copy-start(f32[2,128]{1,0:T(2,128)} %in_bias_ref.1) | copy-start | bytes 3076
  0.8 0.7 %copy-start.6 = (f32[2,128]{1,0:T(2,128)S(1)}, f32[2,128]{1,0:T(2,128)}, u32[]{:S(2)}) copy-start(f32[2,128]{1,0:T(2,128)} %out_gain_ref.1) | copy-start | bytes 3076
  0.8 0.7 %copy-start.7 = (f32[2,128]{1,0:T(2,128)S(1)}, f32[2,128]{1,0:T(2,128)}, u32[]{:S(2)}) copy-start(f32[2,128]{1,0:T(2,128)} %out_bias_ref.1) | copy-start | bytes 3076
  1.5 1.0 %copy-start = (bf16[24,48,128]{2,1,0:T(8,128)(2,1)S(1)}, bf16[24,48,128]{2,1,0:T(8,128)(2,1)}, u32[]{:S(2)}) copy-start(bf16[24,48,128]{2,1,0:T(8,128)(2,1)} %pair_ref.1) | copy-start | bytes 884740
  2.5 0.9 %copy-start.1 = (bf16[2,4,128,128]{3,2,1,0:T(8,128)(2,1)S(1)}, bf16[2,4,128,128]{3,2,1,0:T(8,128)(2,1)}, u32[]{:S(2)}) copy-start(bf16[2,4,128,128]{3,2,1,0:T(8,128)(2,1)} %w_proj_ref.1) | copy-start | bytes 786436
  3.4 0.8 %copy-start.3 = (bf16[2,128,128]{2,1,0:T(8,128)(2,1)S(1)}, bf16[2,128,128]{2,1,0:T(8,128)(2,1)}, u32[]{:S(2)}) copy-start(bf16[2,128,128]{2,1,0:T(8,128)(2,1)} %w_out_ref.1) | copy-start | bytes 196612

commit v2 on v1

--- a/solution.py
+++ b/solution.py
@@ -104,11 +104,12 @@
 
 
 def fused_kernel(
-    sizes, pair_ref, mask_rows_ref, mask_cols_ref, in_gain_ref, in_bias_ref, w_proj_ref, w_gate_ref,
-    out_gain_ref, out_bias_ref, w_out_ref, out_ref,
-    right_all, left_f32, right_f32, part_f32, part_send, part_recv, left_cut, left_send, left_all,
-    left_blk, tri, pair_1, gate,
-    right_recv_sem, right_fwd_sem, right_sib_sem, part_send_sem, part_recv_sem, left_send_sem, left_recv_sem,
+    sizes, mask_row_ref, mask_ref, pair_hbm, in_gain_ref, in_bias_ref, w_proj_hbm, w_gate_hbm,
+    out_gain_ref, out_bias_ref, w_out_hbm, out_ref,
+    right_all, left_f32, right_f32, part_f32, part_send, part_recv, left_cut, left_send, left_peer,
+    left_all, left_blk, tri, pair_1, gate, pair_ref, w_proj_ref, w_gate_ref, w_out_ref,
+    right_recv_sem, right_fwd_sem, right_sib_sem, part_send_sem, part_recv_sem,
+    left_send_sem, left_recv_sem, left_relay_sem, peer_send_sem, peer_recv_sem, load_sem,
 ):
     rows, cols, cores, half, width = sizes
     blocks = rows * cores
@@ -123,19 +124,25 @@
     channels = pair_ref.shape[-1]
 
     barrier = pltpu.get_barrier_semaphore()
-    for dz in range(rows):
-        for dx in range(cols):
-            for dc in range(cores):
-                if dz or dx or dc:
-                    pl.semaphore_signal(
-                        barrier, inc=1,
-                        device_id={
-                            "row": lax.rem(z + dz, rows),
-                            "col": lax.rem(x + dx, cols),
-                            "chan": lax.rem(c + dc, cores),
-                        },
-                        device_id_type=MESH,
-                    )
+    for device_id in ({"chan": sib}, {"col": 1 - x}):
+        pl.semaphore_signal(barrier, inc=1, device_id=device_id, device_id_type=MESH)
+
+    @pl.when(z > 0)
+    def _():
+        pl.semaphore_signal(barrier, inc=1, device_id={"row": z - 1}, device_id_type=MESH)
+
+    @pl.when(z + 1 < rows)
+    def _():
+        pl.semaphore_signal(barrier, inc=1, device_id={"row": z + 1}, device_id_type=MESH)
+
+    loads = [
+        pltpu.make_async_copy(pair_hbm.at[pl.ds(c * half, half)], pair_ref, load_sem.at[0]),
+        pltpu.make_async_copy(w_proj_hbm, w_proj_ref, load_sem.at[1]),
+        pltpu.make_async_copy(w_gate_hbm, w_gate_ref, load_sem.at[2]),
+        pltpu.make_async_copy(w_out_hbm, w_out_ref, load_sem.at[3]),
+    ]
+    for load in loads:
+        load.start()
 
     def right_copy(layer, zb, cb, send_sem, device_id):
         return pltpu.make_async_remote_copy(
@@ -215,13 +222,15 @@
 
                 to_sib(layer, z + s).wait_send()
 
-    def each_block(layer, work):
+    def each_block(layer, work, after_relay=None):
         work(z, c)
         right_copy(layer, z, sib, right_sib_sem.at[layer, z], {"chan": sib}).wait_recv()
         work(z, sib)
 
         def at_distance(s, _):
             relay(layer, s)
+            if after_relay is not None:
+                after_relay(s)
 
             def one(t, _):
                 zb = z + s * (2 * (t % 2) - 1)
@@ -242,8 +251,16 @@
 
         lax.fori_loop(1, rows, at_distance, 0)
 
-    mask_cols = mask_cols_ref[pl.ds(pl.multiple_of(x * width, 8), width)]
-    mask_tile = mask_rows_ref[pl.ds(me * half, half)] * mask_cols[None]
+    tokens_all = mask_ref.shape[1]
+    lane = lax.broadcasted_iota(jnp.int32, (width, tokens_all), 1)
+    here = lax.broadcasted_iota(jnp.int32, (width, tokens_all), 0) + x * width
+    mask_cols = jnp.sum(
+        jnp.where(lane == here, mask_ref[...].astype(jnp.float32), 0.0), axis=1, keepdims=True
+    )
+    mask_cols = jnp.broadcast_to(mask_cols, (width, channels))
+    mask_tile = jnp.stack(
+        [mask_cols * mask_row_ref[0, me * half + r].astype(jnp.float32) for r in range(half)]
+    )
 
     def gated(normed, layer, which):
         opened = jax.nn.sigmoid(dot_f32(normed, w_proj_ref[layer, which]))
@@ -257,13 +274,18 @@
         )
         return pair_now + gate[...] * dot_f32(unit, w_out_ref[layer])
 
-    pair_0 = pair_ref[pl.ds(c * half, half)].astype(jnp.float32).reshape(tokens, channels)
+    loads[0].wait()
+    pair_0 = pair_ref[...].astype(jnp.float32).reshape(tokens, channels)
     normed = fused_norm(pair_0, in_gain_ref[pl.ds(0, 1)], in_bias_ref[pl.ds(0, 1)])
+    loads[1].wait()
     right_all[0, z, c] = gated(normed, 0, 2)
-    pl.semaphore_wait(barrier, blocks * cols - 1)
+    pl.semaphore_wait(barrier, 2 + jnp.minimum(z, 1) + jnp.minimum(rows - 1 - z, 1))
+
     start_right(0)
     left_f32[...] = gated(normed, 0, 0).astype(jnp.float32)
+    loads[2].wait()
     gate[...] = jax.nn.sigmoid(dot_f32(normed, w_gate_ref[0]))
+    loads[3].wait()
 
     def part_copy(q, dx, zb_cb):
         return pltpu.make_async_remote_copy(
@@ -319,28 +341,71 @@
             left_cut[p, k * half:(k + 1) * half] = left_f32[k, p * half:(p + 1) * half]
         left_send[p] = left_cut[p].astype(jnp.bfloat16)
 
-    def left_copy(p, dx):
-        b = x * per_col + p
+    carries = c == x
+    peer = pltpu.make_async_remote_copy(
+        src_ref=left_send, dst_ref=left_peer, send_sem=peer_send_sem, recv_sem=peer_recv_sem,
+        device_id={"col": 1 - x}, device_id_type=MESH,
+    )
+
+    def left_copy(source, p, b):
         return pltpu.make_async_remote_copy(
-            src_ref=left_send.at[p],
+            src_ref=source.at[p],
             dst_ref=left_all.at[me],
-            send_sem=left_send_sem.at[p, dx],
+            send_sem=left_send_sem.at[b],
             recv_sem=left_recv_sem.at[me],
-            device_id={"row": b // cores, "col": dx, "chan": b % cores},
+            device_id={"row": b // cores, "chan": b % cores},
             device_id_type=MESH,
         )
 
-    for p in range(per_col):
-        for dx in range(cols):
-            is_me = (x * per_col + p == me) & (x == dx)
-
-            @pl.when(jnp.logical_not(is_me))
-            def _():
-                left_copy(p, dx).start()
-
-            @pl.when(is_me)
-            def _():
-                left_all[me] = left_send[p]
+    def left_relay(b):
+        return pltpu.make_async_remote_copy(
+            src_ref=left_all.at[b],
+            dst_ref=left_all.at[b],
+            send_sem=left_relay_sem.at[b],
+            recv_sem=left_recv_sem.at[b],
+            device_id={"col": 1 - x},
+            device_id_type=MESH,
+        )
+
+    def send_pieces(source, column):
+        def one(p, _):
+            b = column * per_col + p
+
+            @pl.when(b != me)
+            def _():
+                left_copy(source, p, b).start()
+
+            @pl.when(b == me)
+            def _():
+                left_all[me] = source[p]
+                left_relay(me).start()
+
+            return 0
+
+        lax.fori_loop(0, per_col, one, 0)
+
+    def pass_left(zb):
+        left_relay(zb * cores + x).wait_recv()
+        left_relay(zb * cores + x).start()
+
+    def pass_left_at(s):
+        @pl.when(z - s >= 0)
+        def _():
+            pass_left(z - s)
+
+        @pl.when(z + s < rows)
+        def _():
+            pass_left(z + s)
+
+    @pl.when(carries)
+    def _():
+        send_pieces(left_send, x)
+        peer.wait_recv()
+        send_pieces(left_peer, 1 - x)
+
+    @pl.when(jnp.logical_not(carries))
+    def _():
+        peer.start()
 
     gate[...] = jax.nn.sigmoid(dot_f32(normed, w_gate_ref[1]))
     tri[...] = jnp.zeros_like(tri)
@@ -349,13 +414,9 @@
     def incoming(zb, cb):
         b = zb * cores + cb
 
-        @pl.when(jnp.logical_not((b == me) & (x == me // per_col)))
-        def _():
-            pltpu.make_async_remote_copy(
-                src_ref=left_send.at[0], dst_ref=left_all.at[b],
-                send_sem=left_send_sem.at[0, 0], recv_sem=left_recv_sem.at[b],
-                device_id={"chan": sib}, device_id_type=MESH,
-            ).wait_recv()
+        @pl.when(cb != x)
+        def _():
+            left_relay(b).wait_recv()
 
         left_cut[0] = left_all[b].astype(jnp.float32)
         right_f32[...] = right_all[1, zb, cb].astype(jnp.float32)
@@ -369,7 +430,11 @@
             for i in range(step):
                 tri[i0 + i] = sums[i]
 
-    each_block(1, incoming)
+    @pl.when(jnp.logical_not(carries))
+    def _():
+        pass_left(z)
+
+    each_block(1, incoming, pass_left_at)
     out_ref[...] = finish_layer_here(1, pair_1[...]).reshape(half, width, channels)
 
     finish_right(0)
@@ -379,11 +444,19 @@
         def _():
             part_copy(b % per_col, b // per_col, b).wait_send()
 
-    for p in range(per_col):
-        for dx in range(cols):
-            @pl.when(jnp.logical_not((x * per_col + p == me) & (x == dx)))
-            def _():
-                left_copy(p, dx).wait_send()
+    for zb in range(rows):
+        left_relay(zb * cores + x).wait_send()
+
+    @pl.when(carries)
+    def _():
+        for b in range(blocks):
+            @pl.when(b != me)
+            def _():
+                left_copy(left_send, 0, b).wait_send()
+
+    @pl.when(jnp.logical_not(carries))
+    def _():
+        peer.wait_send()
 
 
 def fused_local(
@@ -394,13 +467,16 @@
     per_col = blocks // cols
     cell = half * half
     channels = pair_act.shape[-1]
-    mask_cols = jnp.broadcast_to(res_mask.astype(jnp.float32)[:, None], (res_mask.shape[0], channels))
-    mask_rows = mask_cols[:, None, :]
+    mask_row = res_mask.reshape(1, res_mask.shape[0])
     f32, bf16, dma = jnp.float32, jnp.bfloat16, pltpu.SemaphoreType.DMA
+    vmem, hbm = pltpu.VMEM, pltpu.HBM
     return pl.pallas_call(
         functools.partial(fused_kernel, sizes),
         out_shape=jax.ShapeDtypeStruct((half, width, channels), f32),
-        in_specs=[pl.BlockSpec(memory_space=pltpu.VMEM)] * 10,
+        in_specs=[
+            pl.BlockSpec(memory_space=space)
+            for space in (pltpu.SMEM, vmem, hbm, vmem, vmem, hbm, hbm, vmem, vmem, hbm)
+        ],
         out_specs=pl.BlockSpec(memory_space=pltpu.VMEM),
         scratch_shapes=[
             pltpu.VMEM((2, rows, cores, half, width, channels), bf16),
@@ -411,23 +487,32 @@
             pltpu.VMEM((cols, per_col, cell, channels), bf16),
             pltpu.VMEM((per_col, cell, channels), f32),
             pltpu.VMEM((per_col, cell, channels), bf16),
+            pltpu.VMEM((per_col, cell, channels), bf16),
             pltpu.VMEM((blocks, cell, channels), bf16),
             pltpu.VMEM((half, half, channels), f32),
             pltpu.VMEM((half, width, channels), f32),
             pltpu.VMEM((half * width, channels), f32),
             pltpu.VMEM((half * width, channels), f32),
+            pltpu.VMEM((half, width, channels), bf16),
+            pltpu.VMEM(w_proj.shape, bf16),
+            pltpu.VMEM(w_gate.shape, bf16),
+            pltpu.VMEM(w_out.shape, bf16),
             dma((2, rows, cores)),
             dma((2, rows + 1)),
             dma((2, rows)),
             dma((blocks,)),
             dma((cols, per_col)),
-            dma((per_col, cols)),
             dma((blocks,)),
+            dma((blocks,)),
+            dma((blocks,)),
+            dma(()),
+            dma(()),
+            dma((4,)),
         ],
         compiler_params=pltpu.CompilerParams(
             collective_id=0, has_side_effects=True, vmem_limit_bytes=48 * 1024 * 1024
         ),
-    )(pair_act, mask_rows, mask_cols, in_gain, in_bias, w_proj, w_gate, out_gain, out_bias, w_out)
+    )(mask_row, mask_row, pair_act, in_gain, in_bias, w_proj, w_gate, out_gain, out_bias, w_out)
 
 
 def local_any(
@@ -437,7 +522,7 @@
     half = pair_act.shape[0] // cores
     width = pair_act.shape[1]
     blocks = rows * cores
-    fits = cores == 2 and blocks % cols == 0 and width == half * (blocks // cols)
+    fits = cores == 2 and cols == 2 and blocks % cols == 0 and width == half * (blocks // cols)
     fits = fits and width % 16 == 0 and (half * half) % 16 == 0
     fits = fits and blocks * half * width * pair_act.shape[2] <= 1 << 20
     args = (pair_act, res_mask, in_gain, in_bias, w_proj, w_gate, out_gain, out_bias, w_out)

time: 53.5 us -> 50.2 us (0.938)
  Pallas kernels: 47.7 us -> 42.4 us
  local copies, waits for them, and re-layouts: 4.24 us -> 7.02 us
  other arithmetic: 0.69 us -> 0 us
    pallas_call x1, Pallas kernels: 47.7 us -> 42.4 us  [fused_local(): pl.pallas_call(functools.partial(fused_kernel, sizes), out_shape=jax.Shap...]
    unnamed x17 -> x19, local copies, waits for them, and re-layouts: 4.01 us -> 7.02 us
    convert_element_type x1 -> x0, other arithmetic: 0.69 us -> none  [fused_local(): res_mask.astype(jnp.float32)[:, None]]
where the time goes in v2:
time: 50.2 us; the launch traced here: 49.5 us
  Pallas kernels  42.4 us (84%)
  local copies, waits for them, and re-layouts  7.02 us (14%)
    pallas_call x1, Pallas kernels, fused_local(): pl.pallas_call(functools.partial(fused_kernel, sizes), out_shape=jax.Shap...  42.4 us
    unnamed x19, local copies, waits for them, and re-layouts  7.02 us

profile of v2, /device:TPU:0, one launch (start us, length us, event | category | flops | bytes accessed | tf_op | source)
XLA Modules:
  0.0 49.5 jit_solution(1935949869011056662)
XLA Ops:
  0.0 0.0 copy-start.5
  0.0 0.0 copy-start.4
  0.0 0.7 %copy-done.5 = f32[2,128]{1,0:T(2,128)S(1)} copy-done((f32[2,128]{1,0:T(2,128)S(1)}, f32[2,128]{1,0:T(2,128)}, u32[]{:S(2)}) %copy-start.5) | copy-done | bytes 1048
  0.7 0.0 copy-done.4
  0.7 0.0 copy-start
  0.7 1.0 %copy-done = bf16[24,48,128]{2,1,0:T(8,128)(2,1)S(1)} copy-done((bf16[24,48,128]{2,1,0:T(8,128)(2,1)S(1)}, bf16[24,48,128]{2,1,0:T(8,128)(2,1)}, u32[]{:S(2)}) %copy-start) | copy-done | bytes 294936
  1.6 0.0 copy-start.1
  1.6 0.9 %copy-done.1 = bf16[2,4,128,128]{3,2,1,0:T(8,128)(2,1)S(1)} copy-done((bf16[2,4,128,128]{3,2,1,0:T(8,128)(2,1)S(1)}, bf16[2,4,128,128]{3,2,1,0:T(8,128)(2,1)}, u32[]{:S(2)}) %copy-start.1) | copy-done | bytes 262168
  2.6 0.0 copy-start.2
  2.6 0.8 %copy-done.2 = bf16[2,128,128]{2,1,0:T(8,128)(2,1)S(1)} copy-done((bf16[2,128,128]{2,1,0:T(8,128)(2,1)S(1)}, bf16[2,128,128]{2,1,0:T(8,128)(2,1)}, u32[]{:S(2)}) %copy-start.2) | copy-done | bytes 65560
  3.4 0.0 copy-start.3
  3.4 0.8 %copy-done.3 = bf16[2,128,128]{2,1,0:T(8,128)(2,1)S(1)} copy-done((bf16[2,128,128]{2,1,0:T(8,128)(2,1)S(1)}, bf16[2,128,128]{2,1,0:T(8,128)(2,1)}, u32[]{:S(2)}) %copy-start.3) | copy-done | bytes 65560
  4.3 0.0 copy-start.6
  4.3 0.7 %copy-done.6 = f32[2,128]{1,0:T(2,128)S(1)} copy-done((f32[2,128]{1,0:T(2,128)S(1)}, f32[2,128]{1,0:T(2,128)}, u32[]{:S(2)}) %copy-start.6) | copy-done | bytes 1048
  5.0 0.0 copy-start.7
  5.0 0.7 %copy-done.7 = f32[2,128]{1,0:T(2,128)S(1)} copy-done((f32[2,128]{1,0:T(2,128)S(1)}, f32[2,128]{1,0:T(2,128)}, u32[]{:S(2)}) %copy-start.7) | copy-done | bytes 1048
  5.6 0.0 copy-start.8
  5.6 0.7 %copy-done.8 = f32[2,128]{1,0:T(2,128)S(1)} copy-done((f32[2,128]{1,0:T(2,128)S(1)}, f32[2,128]{1,0:T(2,128)}, u32[]{:S(2)}) %copy-start.8) | copy-done | bytes 1048
  6.3 42.4 %shard_map.91 = f32[12,48,128]{2,1,0:T(8,128)S(1)} custom-call(s32[1,96]{1,0:T(1,128)S(1)} %bitcast.1, s32[1,96]{1,0:T(1,128)S(1)} %bitcast.2, bf16[24,48,128]{2,1,0:T(8,128)(2,1)S(1)} %copy-done, f32[2,128]{1,0:T(2,128)S(1)} %copy-done.5, f32[2,128]{1,0:T(2,128)S(1)} %copy-done.6, bf16[2,4,128,128]{3,2,1,0:T(8,128)(2,1)S(1)} %copy-done.1, ...), custom_call_target="tpu_custom_call" | custom-call | tf_op jit(solution)/shard_map/pallas_call | solution.py:473
  48.8 0.7 %copy.11 = f32[12,48,128]{2,1,0:T(8,128)} copy(f32[12,48,128]{2,1,0:T(8,128)S(1)} %shard_map.91) | data formatting | bytes 589824
Async XLA Ops:
  0.0 0.7 %copy-start.5 = (f32[2,128]{1,0:T(2,128)S(1)}, f32[2,128]{1,0:T(2,128)}, u32[]{:S(2)}) copy-start(f32[2,128]{1,0:T(2,128)} %in_gain_ref.1) | copy-start | bytes 3076
  0.0 0.7 %copy-start.4 = (s32[96]{0:T(128)S(1)}, s32[96]{0:T(128)}, u32[]{:S(2)}) copy-start(s32[96]{0:T(128)} %param.10) | copy-start | bytes 1156
  0.7 1.0 %copy-start = (bf16[24,48,128]{2,1,0:T(8,128)(2,1)S(1)}, bf16[24,48,128]{2,1,0:T(8,128)(2,1)}, u32[]{:S(2)}) copy-start(bf16[24,48,128]{2,1,0:T(8,128)(2,1)} %pair_hbm.1) | copy-start | bytes 884740
  1.6 0.9 %copy-start.1 = (bf16[2,4,128,128]{3,2,1,0:T(8,128)(2,1)S(1)}, bf16[2,4,128,128]{3,2,1,0:T(8,128)(2,1)}, u32[]{:S(2)}) copy-start(bf16[2,4,128,128]{3,2,1,0:T(8,128)(2,1)} %w_proj_hbm.1) | copy-start | bytes 786436
  2.6 0.8 %copy-start.2 = (bf16[2,128,128]{2,1,0:T(8,128)(2,1)S(1)}, bf16[2,128,128]{2,1,0:T(8,128)(2,1)}, u32[]{:S(2)}) copy-start(bf16[2,128,128]{2,1,0:T(8,128)(2,1)} %w_gate_hbm.1) | copy-start | bytes 196612
  3.4 0.8 %copy-start.3 = (bf16[2,128,128]{2,1,0:T(8,128)(2,1)S(1)}, bf16[2,128,128]{2,1,0:T(8,128)(2,1)}, u32[]{:S(2)}) copy-start(bf16[2,128,128]{2,1,0:T(8,128)(2,1)} %w_out_hbm.1) | copy-start | bytes 196612
  4.3 0.7 %copy-start.6 = (f32[2,128]{1,0:T(2,128)S(1)}, f32[2,128]{1,0:T(2,128)}, u32[]{:S(2)}) copy-start(f32[2,128]{1,0:T(2,128)} %in_bias_ref.1) | copy-start | bytes 3076
  5.0 0.7 %copy-start.7 = (f32[2,128]{1,0:T(2,128)S(1)}, f32[2,128]{1,0:T(2,128)}, u32[]{:S(2)}) copy-start(f32[2,128]{1,0:T(2,128)} %out_gain_ref.1) | copy-start | bytes 3076
  5.6 0.7 %copy-start.8 = (f32[2,128]{1,0:T(2,128)S(1)}, f32[2,128]{1,0:T(2,128)}, u32[]{:S(2)}) copy-start(f32[2,128]{1,0:T(2,128)} %out_bias_ref.1) | copy-start | bytes 3076

commit v3 on v2

--- a/solution.py
+++ b/solution.py
@@ -103,6 +103,10 @@
     return jnp.dot(a, b, preferred_element_type=jnp.float32)
 
 
+def right_chunks(half):
+    return 2 if half % 2 == 0 else 1
+
+
 def fused_kernel(
     sizes, mask_row_ref, mask_ref, pair_hbm, in_gain_ref, in_bias_ref, w_proj_hbm, w_gate_hbm,
     out_gain_ref, out_bias_ref, w_out_hbm, out_ref,
@@ -115,6 +119,7 @@
     blocks = rows * cores
     per_col = blocks // cols
     tokens = half * width
+    chunks = right_chunks(half)
     cell = half * half
     z = lax.axis_index("row")
     x = lax.axis_index("col")
@@ -144,88 +149,101 @@
     for load in loads:
         load.start()
 
-    def right_copy(layer, zb, cb, send_sem, device_id):
+    chunk = half // chunks
+
+    def right_copy(layer, zb, cb, h, send_sem, device_id):
+        part = right_all.at[layer, zb, cb, pl.ds(h * chunk, chunk)]
         return pltpu.make_async_remote_copy(
-            src_ref=right_all.at[layer, zb, cb],
-            dst_ref=right_all.at[layer, zb, cb],
+            src_ref=part,
+            dst_ref=part,
             send_sem=send_sem,
-            recv_sem=right_recv_sem.at[layer, zb, cb],
+            recv_sem=right_recv_sem.at[layer, zb, cb, h],
             device_id=device_id,
             device_id_type=MESH,
         )
 
-    def fwd_right(layer, zb):
-        return right_copy(layer, zb, c, right_fwd_sem.at[layer, zb], {"row": z + 1})
-
-    def fwd_left(layer, zb, slot):
-        return right_copy(layer, zb, c, right_fwd_sem.at[layer, slot], {"row": z - 1})
-
-    def to_sib(layer, zb):
-        return right_copy(layer, zb, c, right_sib_sem.at[layer, zb], {"chan": sib})
+    def fwd_right(layer, zb, h):
+        return right_copy(layer, zb, c, h, right_fwd_sem.at[layer, zb, h], {"row": z + 1})
+
+    def fwd_left(layer, zb, slot, h):
+        return right_copy(layer, zb, c, h, right_fwd_sem.at[layer, slot, h], {"row": z - 1})
+
+    def to_sib(layer, zb, h):
+        return right_copy(layer, zb, c, h, right_sib_sem.at[layer, zb, h], {"chan": sib})
+
+    def wait_right(layer, zb, cb):
+        for h in range(chunks):
+            right_copy(layer, zb, cb, h, right_sib_sem.at[layer, zb, h], {"chan": sib}).wait_recv()
 
     def start_right(layer):
-        @pl.when(z + 1 < rows)
-        def _():
-            fwd_right(layer, z).start()
-
-        @pl.when(z > 0)
-        def _():
-            fwd_left(layer, z, rows).start()
-
-        to_sib(layer, z).start()
+        for h in range(chunks):
+            @pl.when(z + 1 < rows)
+            def _():
+                fwd_right(layer, z, h).start()
+
+            @pl.when(z > 0)
+            def _():
+                fwd_left(layer, z, rows, h).start()
+
+        for h in range(chunks):
+            to_sib(layer, z, h).start()
 
     def relay(layer, s):
-        @pl.when(z - s >= 0)
-        def _():
-            right_copy(layer, z - s, c, right_sib_sem.at[layer, z - s], {"chan": sib}).wait_recv()
-
-            @pl.when(z + 1 < rows)
-            def _():
-                fwd_right(layer, z - s).start()
-
-            to_sib(layer, z - s).start()
-
-        @pl.when(z + s < rows)
-        def _():
-            right_copy(layer, z + s, c, right_sib_sem.at[layer, z + s], {"chan": sib}).wait_recv()
-
-            @pl.when(z > 0)
-            def _():
-                fwd_left(layer, z + s, z + s).start()
-
-            to_sib(layer, z + s).start()
-
-    def finish_right(layer):
-        @pl.when(z + 1 < rows)
-        def _():
-            fwd_right(layer, z).wait_send()
-
-        @pl.when(z > 0)
-        def _():
-            fwd_left(layer, z, rows).wait_send()
-
-        to_sib(layer, z).wait_send()
-        for s in range(1, rows):
+        for h in range(chunks):
             @pl.when(z - s >= 0)
             def _():
+                to_sib(layer, z - s, h).wait_recv()
+
                 @pl.when(z + 1 < rows)
                 def _():
-                    fwd_right(layer, z - s).wait_send()
-
-                to_sib(layer, z - s).wait_send()
+                    fwd_right(layer, z - s, h).start()
+
+                to_sib(layer, z - s, h).start()
 
             @pl.when(z + s < rows)
             def _():
+                to_sib(layer, z + s, h).wait_recv()
+
                 @pl.when(z > 0)
                 def _():
-                    fwd_left(layer, z + s, z + s).wait_send()
-
-                to_sib(layer, z + s).wait_send()
+                    fwd_left(layer, z + s, z + s, h).start()
+
+                to_sib(layer, z + s, h).start()
+
+    def finish_right(layer):
+        def one(h, _):
+            @pl.when(z + 1 < rows)
+            def _():
+                fwd_right(layer, z, h).wait_send()
+
+            @pl.when(z > 0)
+            def _():
+                fwd_left(layer, z, rows, h).wait_send()
+
+            to_sib(layer, z, h).wait_send()
+            for s in range(1, rows):
+                @pl.when(z - s >= 0)
+                def _():
+                    @pl.when(z + 1 < rows)
+                    def _():
+                        fwd_right(layer, z - s, h).wait_send()
+
+                    to_sib(layer, z - s, h).wait_send()
+
+                @pl.when(z + s < rows)
+                def _():
+                    @pl.when(z > 0)
+                    def _():
+                        fwd_left(layer, z + s, z + s, h).wait_send()
+
+                    to_sib(layer, z + s, h).wait_send()
+
+            return 0
+
+        lax.fori_loop(0, chunks, one, 0)
 
     def each_block(layer, work, after_relay=None):
         work(z, c)
-        right_copy(layer, z, sib, right_sib_sem.at[layer, z], {"chan": sib}).wait_recv()
-        work(z, sib)
 
         def at_distance(s, _):
             relay(layer, s)
@@ -233,14 +251,16 @@
                 after_relay(s)
 
             def one(t, _):
-                zb = z + s * (2 * (t % 2) - 1)
-                cb = (c + t // 2) % 2
-
-                @pl.when((zb >= 0) & (zb < rows))
+                own = t // 2
+                far = s - 1 + own
+                zb = z + far * (1 - 2 * (t % 2))
+                cb = (c + 1 - own) % 2
+
+                @pl.when((zb >= 0) & (zb < rows) & ((far > 0) | (t % 2 == 0)))
                 def _():
-                    @pl.when(t >= 2)
+                    @pl.when(own == 0)
                     def _():
-                        right_copy(layer, zb, cb, right_sib_sem.at[layer, zb], {"chan": sib}).wait_recv()
+                        wait_right(layer, zb, cb)
 
                     work(zb, cb)
 
@@ -249,7 +269,7 @@
             lax.fori_loop(0, 4, one, 0)
             return 0
 
-        lax.fori_loop(1, rows, at_distance, 0)
+        lax.fori_loop(1, rows + 1, at_distance, 0)
 
     tokens_all = mask_ref.shape[1]
     lane = lax.broadcasted_iota(jnp.int32, (width, tokens_all), 1)
@@ -468,6 +488,7 @@
     cell = half * half
     channels = pair_act.shape[-1]
     mask_row = res_mask.reshape(1, res_mask.shape[0])
+    chunks = right_chunks(half)
     f32, bf16, dma = jnp.float32, jnp.bfloat16, pltpu.SemaphoreType.DMA
     vmem, hbm = pltpu.VMEM, pltpu.HBM
     return pl.pallas_call(
@@ -497,9 +518,9 @@
             pltpu.VMEM(w_proj.shape, bf16),
             pltpu.VMEM(w_gate.shape, bf16),
             pltpu.VMEM(w_out.shape, bf16),
-            dma((2, rows, cores)),
-            dma((2, rows + 1)),
-            dma((2, rows)),
+            dma((2, rows, cores, chunks)),
+            dma((2, rows + 1, chunks)),
+            dma((2, rows, chunks)),
             dma((blocks,)),
             dma((cols, per_col)),
             dma((blocks,)),
@@ -510,7 +531,7 @@
             dma((4,)),
         ],
         compiler_params=pltpu.CompilerParams(
-            collective_id=0, has_side_effects=True, vmem_limit_bytes=48 * 1024 * 1024
+            collective_id=0, has_side_effects=True, vmem_limit_bytes=64 * 1024 * 1024
         ),
     )(mask_row, mask_row, pair_act, in_gain, in_bias, w_proj, w_gate, out_gain, out_bias, w_out)
 

time: 50.2 us -> 43.2 us (0.86); the launches traced: 49.5 us -> 43 us
  local copies, waits for them, and re-layouts: 7.02 us -> 1.69 us
  Pallas kernels: 42.4 us -> 41.3 us
    unnamed x19 -> x1, local copies, waits for them, and re-layouts: 7.02 us -> 1.69 us
    pallas_call x1, Pallas kernels: 42.4 us -> 41.3 us  [fused_local(): pl.pallas_call(functools.partial(fused_kernel, sizes), out_shape=jax.Shap...]
where the time goes in v3:
time: 43.2 us; the launch traced here: 43 us
  Pallas kernels  41.3 us (96%)
  local copies, waits for them, and re-layouts  1.69 us (4%)
    pallas_call x1, Pallas kernels, fused_local(): pl.pallas_call(functools.partial(fused_kernel, sizes), out_shape=jax.Shap...  41.3 us
    unnamed x1, local copies, waits for them, and re-layouts  1.69 us

profile of v3, /device:TPU:0, one launch (start us, length us, event | category | flops | bytes accessed | tf_op | source)
XLA Modules:
  0.0 43.0 jit_solution(1833030095585215975)
XLA Ops:
  0.0 41.3 %shard_map.91 = f32[12,48,128]{2,1,0:T(8,128)} custom-call(s32[1,96]{1,0:T(1,128)} %bitcast.1, s32[1,96]{1,0:T(1,128)} %bitcast.2, bf16[24,48,128]{2,1,0:T(8,128)(2,1)} %pair_hbm.1, f32[2,128]{1,0:T(2,128)} %in_gain_ref.1, f32[2,128]{1,0:T(2,128)} %in_bias_ref.1, bf16[2,4,128,128]{3,2,1,0:T(8,128)(2,1)} %w_proj_hbm.1, bf16[2,128,128]{2,1,0:T(8,128)(2,1)} %w_gate_hbm.1, ...), custom_call_target="tpu_custom_call" | custom-call | tf_op jit(solution)/shard_map/pallas_call | solution.py:494
  41.3 1.7 %copy.11 = f32[12,48,128]{2,1,0:T(8,128)} copy(f32[12,48,128]{2,1,0:T(8,128)} %shard_map.91) | data formatting | bytes 589824

commit v4 on v3

--- a/solution.py
+++ b/solution.py
@@ -104,14 +104,15 @@
 
 
 def right_chunks(half):
-    return 2 if half % 2 == 0 else 1
+    return 3 if half % 3 == 0 else 1
 
 
 def fused_kernel(
-    sizes, mask_row_ref, mask_ref, pair_hbm, in_gain_ref, in_bias_ref, w_proj_hbm, w_gate_hbm,
-    out_gain_ref, out_bias_ref, w_out_hbm, out_ref,
+    sizes, mask_row_ref, mask_hbm, pair_hbm, in_gain_hbm, in_bias_hbm, w_proj_hbm, w_gate_hbm,
+    out_gain_hbm, out_bias_hbm, w_out_hbm, out_ref,
     right_all, left_f32, right_f32, part_f32, part_send, part_recv, left_cut, left_send, left_peer,
     left_all, left_blk, tri, pair_1, gate, pair_ref, w_proj_ref, w_gate_ref, w_out_ref,
+    mask_ref, in_gain_ref, in_bias_ref, out_gain_ref, out_bias_ref,
     right_recv_sem, right_fwd_sem, right_sib_sem, part_send_sem, part_recv_sem,
     left_send_sem, left_recv_sem, left_relay_sem, peer_send_sem, peer_recv_sem, load_sem,
 ):
@@ -145,6 +146,11 @@
         pltpu.make_async_copy(w_proj_hbm, w_proj_ref, load_sem.at[1]),
         pltpu.make_async_copy(w_gate_hbm, w_gate_ref, load_sem.at[2]),
         pltpu.make_async_copy(w_out_hbm, w_out_ref, load_sem.at[3]),
+        pltpu.make_async_copy(in_gain_hbm, in_gain_ref, load_sem.at[4]),
+        pltpu.make_async_copy(in_bias_hbm, in_bias_ref, load_sem.at[5]),
+        pltpu.make_async_copy(mask_hbm, mask_ref, load_sem.at[6]),
+        pltpu.make_async_copy(out_gain_hbm, out_gain_ref, load_sem.at[7]),
+        pltpu.make_async_copy(out_bias_hbm, out_bias_ref, load_sem.at[8]),
     ]
     for load in loads:
         load.start()
@@ -272,6 +278,7 @@
         lax.fori_loop(1, rows + 1, at_distance, 0)
 
     tokens_all = mask_ref.shape[1]
+    loads[6].wait()
     lane = lax.broadcasted_iota(jnp.int32, (width, tokens_all), 1)
     here = lax.broadcasted_iota(jnp.int32, (width, tokens_all), 0) + x * width
     mask_cols = jnp.sum(
@@ -294,7 +301,8 @@
         )
         return pair_now + gate[...] * dot_f32(unit, w_out_ref[layer])
 
-    loads[0].wait()
+    for n in (0, 4, 5):
+        loads[n].wait()
     pair_0 = pair_ref[...].astype(jnp.float32).reshape(tokens, channels)
     normed = fused_norm(pair_0, in_gain_ref[pl.ds(0, 1)], in_bias_ref[pl.ds(0, 1)])
     loads[1].wait()
@@ -305,7 +313,8 @@
     left_f32[...] = gated(normed, 0, 0).astype(jnp.float32)
     loads[2].wait()
     gate[...] = jax.nn.sigmoid(dot_f32(normed, w_gate_ref[0]))
-    loads[3].wait()
+    for n in (3, 7, 8):
+        loads[n].wait()
 
     def part_copy(q, dx, zb_cb):
         return pltpu.make_async_remote_copy(
@@ -429,7 +438,7 @@
 
     gate[...] = jax.nn.sigmoid(dot_f32(normed, w_gate_ref[1]))
     tri[...] = jnp.zeros_like(tri)
-    step = 4 if half % 4 == 0 else 1
+    step = 6 if half % 6 == 0 else 1
 
     def incoming(zb, cb):
         b = zb * cores + cb
@@ -496,7 +505,7 @@
         out_shape=jax.ShapeDtypeStruct((half, width, channels), f32),
         in_specs=[
             pl.BlockSpec(memory_space=space)
-            for space in (pltpu.SMEM, vmem, hbm, vmem, vmem, hbm, hbm, vmem, vmem, hbm)
+            for space in (pltpu.SMEM,) + (hbm,) * 9
         ],
         out_specs=pl.BlockSpec(memory_space=pltpu.VMEM),
         scratch_shapes=[
@@ -518,6 +527,11 @@
             pltpu.VMEM(w_proj.shape, bf16),
             pltpu.VMEM(w_gate.shape, bf16),
             pltpu.VMEM(w_out.shape, bf16),
+            pltpu.VMEM(mask_row.shape, jnp.int32),
+            pltpu.VMEM(in_gain.shape, f32),
+            pltpu.VMEM(in_gain.shape, f32),
+            pltpu.VMEM(in_gain.shape, f32),
+            pltpu.VMEM(in_gain.shape, f32),
             dma((2, rows, cores, chunks)),
             dma((2, rows + 1, chunks)),
             dma((2, rows, chunks)),
@@ -528,7 +542,7 @@
             dma((blocks,)),
             dma(()),
             dma(()),
-            dma((4,)),
+            dma((9,)),
         ],
         compiler_params=pltpu.CompilerParams(
             collective_id=0, has_side_effects=True, vmem_limit_bytes=64 * 1024 * 1024

time: 43.2 us -> 43.1 us (level)
  no operation moved by 1% of the time
where the time goes in v4:
time: 43.1 us; the launch traced here: 42.9 us
  Pallas kernels  41.2 us (96%)
  local copies, waits for them, and re-layouts  1.69 us (4%)
    pallas_call x1, Pallas kernels, fused_local(): pl.pallas_call(functools.partial(fused_kernel, sizes), out_shape=jax.Shap...  41.2 us
    unnamed x1, local copies, waits for them, and re-layouts  1.69 us

profile of v4, /device:TPU:0, one launch (start us, length us, event | category | flops | bytes accessed | tf_op | source)
XLA Modules:
  0.0 42.9 jit_solution(17293089915676652084)
XLA Ops:
  0.0 41.2 %shard_map.91 = f32[12,48,128]{2,1,0:T(8,128)} custom-call(s32[1,96]{1,0:T(1,128)} %bitcast.1, s32[1,96]{1,0:T(1,128)} %bitcast.2, bf16[24,48,128]{2,1,0:T(8,128)(2,1)} %pair_hbm.1, f32[2,128]{1,0:T(2,128)} %in_gain_hbm.1, f32[2,128]{1,0:T(2,128)} %in_bias_hbm.1, bf16[2,4,128,128]{3,2,1,0:T(8,128)(2,1)} %w_proj_hbm.1, bf16[2,128,128]{2,1,0:T(8,128)(2,1)} %w_gate_hbm.1, ...), custom_call_target="tpu_custom_call" | custom-call | tf_op jit(solution)/shard_map/pallas_call | solution.py:503
  41.2 1.7 %copy.11 = f32[12,48,128]{2,1,0:T(8,128)} copy(f32[12,48,128]{2,1,0:T(8,128)} %shard_map.91) | data formatting | bytes 589824
